TPU v7x, 32 devices: a whole 2x2x4 slice. The times are simulated.
32 devices in a mesh: groups: 2 (over y), row: 4 (over z), col: 2 (over x), sub: 2 (over core).
Axes of the slice: x: 2, y: 2, z: 4, core: 2. Of those that a mesh axis runs over, the one named last changes fastest.
Arguments:
- pixels: bfloat16 [4, 4096, 2048], P('groups', ('row', 'col', 'sub')), parts along dimension 0, may hold values from 0.019897461 to 1
Outputs:
- phase: float32 [4, 512, 256], P(('groups', 'sub'), 'row', 'col'), parts along dimension 0
- mean_flux: float32 [4, 512, 256], P(('groups', 'sub'), 'row', 'col'), parts along dimension 0
- spot_size: float32 [4, 512, 256], P(('groups', 'sub'), 'row', 'col'), parts along dimension 0
There are 2 independent parts, one for each index of `groups`. A program takes and returns all parts, laid end to end along the dimension named above; each array names one. Nothing has to cross between parts.
All inputs are finite; a program needn't handle non-finite values.
Results may differ from a plain program's by a relative error of at most 0.0011.
Values sent between devices are 32-bit elements; how exact they have to be, the bound alone decides.
A program may use at most 128 MiB of HBM per device.

v0:
```python
import functools
import math

import jax
import jax.numpy as jnp
import numpy as np
from jax import lax
from jax.experimental import pallas as pl
from jax.experimental.pallas import tpu as pltpu
from jax.sharding import PartitionSpec as P

PIX = 8
SUBN = 128
MARGIN = 8
SIDE = SUBN + 2 * MARGIN
damping = 2e-05
MESH = pl.DeviceIdType.MESH


def split_bf16(values):
    high = values.astype(jnp.bfloat16)
    return high, (values - high.astype(jnp.float32)).astype(jnp.bfloat16)


def dot(left, right, contract=((1,), (0,))):
    return lax.dot_general(left, right, (contract, ((), ())), preferred_element_type=jnp.float32)


def dot_three(left, right, contract=((1,), (0,))):
    (left_high, left_low), (right_high, right_low) = left, right
    return (
        dot(left_high, right_high, contract)
        + dot(left_low, right_high, contract)
        + dot(left_high, right_low, contract)
    )


def host_tables():
    order = np.arange(1, SIDE + 1, dtype=np.float64)
    vectors = np.sqrt(2.0 / (SIDE + 1)) * np.sin(math.pi * np.outer(order, order) / (SIDE + 1))
    spectrum = 2.0 - 2.0 * np.cos(math.pi * order / (SIDE + 1))
    inverse = 1.0 / (spectrum[:, None] + spectrum[None, :] + damping)
    corner = np.zeros((SIDE, SUBN))
    corner[:, :MARGIN] = vectors[:, SUBN + MARGIN :]
    corner[:, SUBN - MARGIN :] = vectors[:, :MARGIN]
    last = np.concatenate([vectors[:, MARGIN : MARGIN + SUBN], corner], 1)
    rims = np.concatenate([vectors[:MARGIN], vectors[SUBN + MARGIN :]], 0)
    wide = [np.pad(part, ((0, 0), (0, 2 * SUBN - part.shape[1]))) for part in (vectors, inverse, rims)]
    return np.concatenate([wide[0], last, wide[1], wide[2]], 0).astype(np.float32)


def coarse_inverse(blocks_down, blocks_across):
    number = blocks_down * blocks_across
    labels = np.arange(number)
    down, across = labels // blocks_across, labels % blocks_across
    apart = np.abs(down[:, None] - down[None, :]) + np.abs(across[:, None] - across[None, :])
    touching = (apart == 1).astype(np.float64)
    laplace = np.diag(touching.sum(1)) - touching
    matrix = SUBN * laplace + damping * SUBN * SUBN * np.eye(number)
    root = np.linalg.inv(np.linalg.cholesky(matrix))
    spare = max(SUBN - number, 0)
    return np.pad(root.T @ root, ((0, 0), (0, spare))).astype(np.float32)


def each(count, step):
    if count <= 16:
        for index in range(1, count):
            step(index)
    else:
        pl.loop(1, count)(step)


def kernel(
    sizes,
    pixels,
    constants,
    phase,
    flux,
    spot,
    loaded,
    tables,
    halves,
    coarse,
    pick_one,
    pick_two,
    parts,
    extras,
    stripes,
    above,
    below,
    second,
    sums,
    rim_out,
    row_out,
    side_in,
    row_in,
    load_sem,
    table_sem,
    part_sem,
    extra_sem,
    edge_sem,
    sum_sem,
    fold_sem,
):
    rows, cols, cores = sizes
    frames, pixel_rows, pixel_cols = pixels.shape
    high = pixel_rows // PIX
    wide = pixel_cols // PIX
    team = cols * cores
    blocks = rows * cols
    chunk = SUBN * PIX
    row, col, core = (lax.axis_index(name) for name in ("row", "col", "sub"))
    seat = col * cores + core
    block = row * cols + col

    def load(frame, tile):
        lanes = pl.ds(tile * chunk, chunk)
        return pltpu.make_async_copy(
            pixels.at[frame, :, lanes], loaded.at[frame, :, lanes], load_sem.at[frame, tile]
        )

    for frame in range(frames):
        for tile in range(cols):
            load(frame, tile).start()
    fetches = [
        pltpu.make_async_copy(far, near, table_sem.at[index])
        for index, (far, near) in enumerate(
            (
                (constants.at[pl.ds(0, tables.shape[0])], tables),
                (
                    constants.at[
                        pl.ds(tables.shape[0], coarse.shape[0]), pl.ds(0, coarse.shape[1])
                    ],
                    coarse,
                ),
            )
        )
    ]
    for copy in fetches:
        copy.start()

    for ref in (above, below, second, side_in, row_in):
        ref[...] = jnp.zeros_like(ref)

    barrier = pltpu.get_barrier_semaphore()
    everyone = rows * team
    here = row * team + seat

    def greet(step):
        other = lax.rem(here + step, everyone)
        pl.semaphore_signal(
            barrier,
            inc=1,
            device_id={
                "row": other // team,
                "col": lax.rem(other, team) // cores,
                "sub": lax.rem(other, cores),
            },
            device_id_type=MESH,
        )

    each(everyone, greet)

    pixel = lax.broadcasted_iota(jnp.int32, (chunk, SUBN), 0)
    lane = lax.broadcasted_iota(jnp.int32, (chunk, SUBN), 1)
    inside = (pixel >> 3) == lane
    offset = (pixel & 7).astype(jnp.float32) - (PIX - 1) / 2.0
    pick_one[...] = jnp.where(inside, 1.0, 0.0).astype(jnp.bfloat16)
    pick_two[:, :SUBN] = jnp.where(inside, offset, 0.0).astype(jnp.bfloat16)
    pick_two[:, SUBN:] = jnp.where(inside, offset * offset, 0.0).astype(jnp.bfloat16)
    line = lax.broadcasted_iota(jnp.int32, (high, pixel_rows), 0)
    pixel = lax.broadcasted_iota(jnp.int32, (high, pixel_rows), 1)
    inside = (pixel >> 3) == line
    offset = (pixel & 7).astype(jnp.float32) - (PIX - 1) / 2.0
    gather = jnp.concatenate(
        [
            jnp.where(inside, 1.0, 0.0),
            jnp.where(inside, offset, 0.0),
            jnp.where(inside, offset * offset, 0.0),
        ],
        0,
    ).astype(jnp.bfloat16)

    def window(across):
        return pl.ds(pl.multiple_of(across * SUBN, SUBN), 2 * SUBN)

    def square(across):
        return pl.ds(pl.multiple_of(across * SUBN, SUBN), SUBN)

    def part_copy(frame, across):
        return pltpu.make_async_remote_copy(
            src_ref=parts.at[frame, :, window(across)],
            dst_ref=stripes.at[seat],
            send_sem=part_sem.at[0, frame, across],
            recv_sem=part_sem.at[1, core, col],
            device_id={"col": across, "sub": frame},
            device_id_type=MESH,
        )

    own_lines = pl.ds(pl.multiple_of(seat * high, 8), high)

    def extra_copy(kind, frame, across):
        return pltpu.make_async_remote_copy(
            src_ref=extras.at[frame, kind, :, square(across)],
            dst_ref=(flux, spot)[kind].at[0, own_lines, :],
            send_sem=extra_sem.at[kind, 0, frame, across],
            recv_sem=extra_sem.at[kind, 1, core, col],
            device_id={"col": across, "sub": frame},
            device_id_type=MESH,
        )

    def edge_copy(which, frame, across):
        lines = (
            pl.ds(0, MARGIN),
            pl.ds(high - MARGIN, 2 * MARGIN),
            pl.ds(high, MARGIN),
        )[which]
        return pltpu.make_async_remote_copy(
            src_ref=parts.at[frame, lines, window(across)],
            dst_ref=(below, above, second)[which],
            send_sem=edge_sem.at[which, 0, frame, across],
            recv_sem=edge_sem.at[which, 1, 0, 0],
            device_id={"row": row + (-1 if which == 0 else 1), "col": across, "sub": frame},
            device_id_type=MESH,
        )

    edges = [
        (0, (seat == 0) & (row > 0), row < rows - 1),
        (1, (seat == team - 1) & (row < rows - 1), row > 0),
    ]
    if high == MARGIN:
        edges.append((2, (seat == team - 2) & (row < rows - 1), row > 0))

    def members(frame, action):
        for step in range(1, cols):
            action(lax.rem(col + step, cols))
        pl.when(core != frame)(lambda: action(col))

    def senders(action):
        def one(step):
            other = lax.rem(seat + step, team)
            action(lax.rem(other, cores), other // cores)

        each(team, one)

    line = lax.broadcasted_iota(jnp.int32, (high, wide), 0)
    column = lax.broadcasted_iota(jnp.int32, (high, wide), 1)
    stripe = row * team + seat
    for frame in range(frames):
        summed = []
        for tile in range(cols):
            load(frame, tile).wait()
            summed.append(dot(gather, loaded[frame, :, tile * chunk : (tile + 1) * chunk]))
        near, far = split_bf16(
            jnp.concatenate(
                [part[kind * high : (kind + 1) * high] for kind in range(3) for part in summed], 0
            )
        )
        tall = cols * high
        ones = dot(near, pick_one[...]) + dot(far, pick_one[...])
        twos = dot(near[:tall], pick_two[...]) + dot(far[:tall], pick_two[...])
        intensity = ones[:tall]
        scale = 1.0 / intensity
        slope_x = twos[:, :SUBN] * scale
        slope_y = ones[tall : 2 * tall] * scale
        moment_two = twos[:, SUBN:] + ones[2 * tall :]

        def grid(values):
            return jnp.concatenate(
                [values[tile * high : (tile + 1) * high] for tile in range(cols)], 1
            )

        flow_x = jnp.where(column < wide - 1, grid(slope_x), 0.0)
        flow_y = jnp.where(stripe * high + line < rows * SUBN - 1, grid(slope_y), 0.0)
        over = pltpu.roll(flow_y, 1, 0)
        source = pltpu.roll(flow_x, 1, 1) - flow_x - flow_y + jnp.where(line > 0, over, 0.0)
        carried = jnp.where(line == 0, over, 0.0)[:MARGIN]
        both = jnp.concatenate([source, carried], 0)
        both = jnp.concatenate([both, jnp.zeros((high + MARGIN, SUBN), jnp.float32)], 1)
        parts[frame] = pltpu.roll(both, MARGIN, 1)
        if frame == 0:
            pl.semaphore_wait(barrier, everyone - 1)
        members(frame, lambda across: part_copy(frame, across).start())
        for which, sends, _ in edges:

            @pl.when(sends)
            def _():
                for across in range(cols):
                    edge_copy(which, frame, across).start()

        extras[frame, 0] = grid(intensity) * (1.0 / (PIX * PIX))
        extras[frame, 1] = grid(moment_two * scale - slope_x * slope_x - slope_y * slope_y)

    for frame in range(frames):
        for kind in range(2):
            members(frame, lambda across: extra_copy(kind, frame, across).start())

    for copy in fetches:
        copy.wait()
    for lines, source_lines in (
        (slice(0, 2 * SIDE), slice(0, 2 * SIDE)),
        (slice(2 * SIDE, 2 * SIDE + 2 * MARGIN), slice(3 * SIDE, 3 * SIDE + 2 * MARGIN)),
    ):
        halves[0, lines], halves[1, lines] = split_bf16(tables[source_lines])

    stripes[seat] = parts[core, :, window(col)]
    flux[0, own_lines, :] = extras[core, 0, :, square(col)]
    spot[0, own_lines, :] = extras[core, 1, :, square(col)]

    def part_arrival(of_core, of_col):
        return pltpu.make_async_remote_copy(
            src_ref=stripes.at[0],
            dst_ref=stripes.at[0],
            send_sem=part_sem.at[0, 0, 0],
            recv_sem=part_sem.at[1, of_core, of_col],
            device_id={"col": of_col, "sub": of_core},
            device_id_type=MESH,
        )

    def extra_arrival(kind, of_core, of_col):
        lines = pl.ds(0, high)
        return pltpu.make_async_remote_copy(
            src_ref=flux.at[0, lines, :],
            dst_ref=(flux, spot)[kind].at[0, lines, :],
            send_sem=extra_sem.at[kind, 0, 0, 0],
            recv_sem=extra_sem.at[kind, 1, of_core, of_col],
            device_id={"col": of_col, "sub": of_core},
            device_id_type=MESH,
        )

    senders(lambda of_core, of_col: part_arrival(of_core, of_col).wait_recv())
    for which, _, receives in edges:

        @pl.when(receives)
        def _():
            edge_copy(which, 0, 0).wait_recv()

    top = above[:MARGIN]
    if high == MARGIN:
        top = top + second[...]
    tiles = [top]
    carry = above[MARGIN:]
    for index in range(team):
        tiles.append(stripes[index, :MARGIN] + carry)
        if high > MARGIN:
            tiles.append(stripes[index, MARGIN:high])
        carry = stripes[index, high:]
    tiles.append(below[...] + carry)
    total = jnp.concatenate(tiles, 0)
    middle = jnp.sum(total[MARGIN : MARGIN + SUBN].reshape(SUBN // 8, 8, 2 * SUBN), 0)
    lane = lax.broadcasted_iota(jnp.int32, (8, SUBN), 1)
    sums[block] = jnp.where(lane < MARGIN, middle[:, SUBN:], middle[:, :SUBN])

    def sum_copy(step):
        to = lax.rem(block + step, blocks)
        return pltpu.make_async_remote_copy(
            src_ref=sums.at[block],
            dst_ref=sums.at[block],
            send_sem=sum_sem.at[0, step],
            recv_sem=sum_sem.at[1, step],
            device_id={"row": to // cols, "col": lax.rem(to, cols)},
            device_id_type=MESH,
        )

    each(blocks, lambda step: sum_copy(step).start())

    vectors, last, rims = (
        (halves[0, lines, :lanes], halves[1, lines, :lanes])
        for lines, lanes in (
            (slice(0, SIDE), SIDE),
            (slice(SIDE, 2 * SIDE), 2 * SUBN),
            (slice(2 * SIDE, 2 * SIDE + 2 * MARGIN), SIDE),
        )
    )
    inverse = tables[2 * SIDE : 3 * SIDE, :SIDE]
    data = split_bf16(total[:, :SIDE])
    data = split_bf16(dot_three(data, vectors))
    data = dot_three(vectors, data) * inverse
    data = split_bf16(dot_three(vectors, split_bf16(data)))
    sides = dot_three(
        rims,
        (data[0][MARGIN : MARGIN + SUBN], data[1][MARGIN : MARGIN + SUBN]),
        ((1,), (1,)),
    )
    rim_out[...] = sides
    solved = dot_three(data, last)
    for index, lines in enumerate((slice(0, MARGIN), slice(SUBN + MARGIN, SIDE))):
        ends = solved[lines, SUBN:]
        row_out[index, 0] = jnp.where(lane >= SUBN - MARGIN, ends, 0.0)
        row_out[index, 1] = solved[lines, :SUBN]
        row_out[index, 2] = jnp.where(lane < MARGIN, ends, 0.0)

    moves = []
    for down in (-1, 0, 1):
        for right in (-1, 0, 1):
            if down == 0 and right == 0:
                continue
            number = (down + 1) * 3 + right + 1
            if down == 0:
                src = rim_out.at[pl.ds(MARGIN if right > 0 else 0, MARGIN)]
                dst = side_in.at[pl.ds(0 if right > 0 else SUBN - MARGIN, MARGIN)]
            else:
                src = row_out.at[(down + 1) // 2, right + 1]
                dst = row_in.at[(down + 1) // 2, right + 1]
            copy = pltpu.make_async_remote_copy(
                src_ref=src,
                dst_ref=dst,
                send_sem=fold_sem.at[0, number],
                recv_sem=fold_sem.at[1, number],
                device_id={"row": row + down, "col": col + right},
                device_id_type=MESH,
            )

            def exists(sign):
                test = row >= 0
                if down:
                    at = row + sign * down
                    test = test & (at >= 0) & (at < rows)
                if right:
                    at = col + sign * right
                    test = test & (at >= 0) & (at < cols)
                return test

            moves.append((copy, exists(1), exists(-1)))

    for copy, sends, _ in moves:
        pl.when(sends)(copy.start)

    each(blocks, lambda step: sum_copy(step).wait_recv())
    mix = sums[0] * coarse[block, 0]
    for index in range(1, blocks):
        mix = mix + sums[index] * coarse[block, index]
    lift = jnp.sum(jnp.sum(mix, 0, keepdims=True), 1, keepdims=True)
    mine = solved[MARGIN : MARGIN + SUBN, :SUBN] + lift

    for copy, _, receives in moves:
        pl.when(receives)(copy.wait_recv)
    mine = mine + side_in[...].T
    phase[0] = jnp.concatenate(
        [
            mine[:MARGIN] + row_in[1, 0] + row_in[1, 1] + row_in[1, 2],
            mine[MARGIN : SUBN - MARGIN],
            mine[SUBN - MARGIN :] + row_in[0, 0] + row_in[0, 1] + row_in[0, 2],
        ],
        0,
    )

    for kind in range(2):
        senders(lambda of_core, of_col: extra_arrival(kind, of_core, of_col).wait_recv())
    for frame in range(frames):
        members(frame, lambda across: part_copy(frame, across).wait_send())
        for kind in range(2):
            members(frame, lambda across: extra_copy(kind, frame, across).wait_send())
        for which, sends, _ in edges:

            @pl.when(sends)
            def _():
                for across in range(cols):
                    edge_copy(which, frame, across).wait_send()

    each(blocks, lambda step: sum_copy(step).wait_send())
    for copy, sends, _ in moves:
        pl.when(sends)(copy.wait_send)


def deliver(phase, flux, spot, phase_out, flux_out, spot_out, sem):
    copies = [
        pltpu.make_async_copy(near, far, sem.at[index])
        for index, (near, far) in enumerate(
            ((phase, phase_out), (flux, flux_out), (spot, spot_out))
        )
    ]
    for copy in copies:
        copy.start()
    for copy in copies:
        copy.wait()


def body(sizes, pixels):
    rows, cols, cores = sizes
    frames, pixel_rows, pixel_cols = pixels.shape
    high = pixel_rows // PIX
    wide = pixel_cols // PIX
    team = cols * cores
    blocks = rows * cols
    vmem = pl.BlockSpec(memory_space=pltpu.VMEM)
    hbm = pl.BlockSpec(memory_space=pltpu.HBM)
    square = jax.ShapeDtypeStruct((1, SUBN, SUBN), jnp.float32)
    tables = host_tables()
    coarse = coarse_inverse(rows, cols)
    constants = np.zeros((2304, 2 * SUBN), np.float32)
    constants[: tables.shape[0]] = tables
    constants[tables.shape[0] : tables.shape[0] + blocks, : coarse.shape[1]] = coarse
    dma = pltpu.SemaphoreType.DMA
    results = pl.pallas_call(
        functools.partial(kernel, sizes),
        out_shape=(square, square, square),
        in_specs=[hbm] * 2,
        out_specs=(vmem, vmem, vmem),
        scratch_shapes=[
            pltpu.VMEM((frames, pixel_rows, pixel_cols), jnp.bfloat16),
            pltpu.VMEM(tables.shape, jnp.float32),
            pltpu.VMEM((2, 2 * SIDE + 2 * MARGIN, 2 * SUBN), jnp.bfloat16),
            pltpu.SMEM(coarse.shape, jnp.float32),
            pltpu.VMEM((SUBN * PIX, SUBN), jnp.bfloat16),
            pltpu.VMEM((SUBN * PIX, 2 * SUBN), jnp.bfloat16),
            pltpu.VMEM((frames, high + MARGIN, wide + SUBN), jnp.float32),
            pltpu.VMEM((frames, 2, high, wide), jnp.float32),
            pltpu.VMEM((team, high + MARGIN, 2 * SUBN), jnp.float32),
            pltpu.VMEM((2 * MARGIN, 2 * SUBN), jnp.float32),
            pltpu.VMEM((MARGIN, 2 * SUBN), jnp.float32),
            pltpu.VMEM((MARGIN, 2 * SUBN), jnp.float32),
            pltpu.VMEM((blocks, 8, SUBN), jnp.float32),
            pltpu.VMEM((2 * MARGIN, SUBN), jnp.float32),
            pltpu.VMEM((2, 3, MARGIN, SUBN), jnp.float32),
            pltpu.VMEM((SUBN, SUBN), jnp.float32),
            pltpu.VMEM((2, 3, MARGIN, SUBN), jnp.float32),
            dma((frames, cols)),
            dma((2,)),
            dma((2, cores, cols)),
            dma((2, 2, cores, cols)),
            dma((3, 2, cores, cols)),
            dma((2, blocks)),
            dma((2, 9)),
        ],
        compiler_params=pltpu.CompilerParams(
            collective_id=0, has_side_effects=True, vmem_limit_bytes=53_000_000
        ),
        name="schwarz",
    )(pixels, constants)
    return pl.pallas_call(
        deliver,
        out_shape=(square, square, square),
        in_specs=[vmem] * 3,
        out_specs=(hbm, hbm, hbm),
        scratch_shapes=[dma((3,))],
        name="deliver",
    )(*results)


def solution(mesh):
    sizes = tuple(mesh.shape[name] for name in ("row", "col", "sub"))
    out = P(("groups", "sub"), "row", "col")
    return jax.shard_map(
        functools.partial(body, sizes),
        mesh=mesh,
        in_specs=(P("groups", ("row", "col", "sub"), None),),
        out_specs=(out, out, out),
        check_vma=False,
    )
```

profile of v0, /device:TPU:1, one launch (start us, length us, event | category | flops | bytes accessed | tf_op | source)
XLA Modules:
  0.0 19.9 jit_solution(9587755435555417163)
XLA Ops:
  0.6 0.0 copy-start
  0.6 1.6 %copy-done = bf16[2,256,2048]{2,1,0:T(8,128)(2,1)S(1)} copy-done((bf16[2,256,2048]{2,1,0:T(8,128)(2,1)S(1)}, bf16[2,256,2048]{2,1,0:T(8,128)(2,1)}, u32[]{:S(2)}) %copy-start) | copy-done | bytes 2097176
  2.2 14.2 %schwarz.1 = (f32[1,128,128]{2,1,0:T(8,128)S(1)}, f32[1,128,128]{2,1,0:T(8,128)S(1)}, f32[1,128,128]{2,1,0:T(8,128)S(1)}) custom-call(bf16[2,256,2048]{2,1,0:T(8,128)(2,1)S(1)} %copy-done, f32[2304,256]{1,0:T(8,128)} %constant.2.clone.constants), custom_call_target="tpu_custom_call" | custom-call | tf_op jit(solution)/shard_map/schwarz/pallas_call | solution.py:495
  16.4 0.0 copy-start.1
  16.4 0.6 %copy-done.1 = f32[1,128,128]{2,1,0:T(8,128)} copy-done((f32[1,128,128]{2,1,0:T(8,128)}, f32[1,128,128]{2,1,0:T(8,128)S(1)}, u32[]{:S(2)}) %copy-start.1) | copy-done | bytes 65560
  17.1 0.0 copy-start.2
  17.1 0.6 %copy-done.2 = f32[1,128,128]{2,1,0:T(8,128)} copy-done((f32[1,128,128]{2,1,0:T(8,128)}, f32[1,128,128]{2,1,0:T(8,128)S(1)}, u32[]{:S(2)}) %copy-start.2) | copy-done | bytes 65560
  17.7 0.0 copy-start.3
  17.7 0.6 %copy-done.3 = f32[1,128,128]{2,1,0:T(8,128)} copy-done((f32[1,128,128]{2,1,0:T(8,128)}, f32[1,128,128]{2,1,0:T(8,128)S(1)}, u32[]{:S(2)}) %copy-start.3) | copy-done | bytes 65560
  18.3 1.6 %deliver.1 = (f32[1,128,128]{2,1,0:T(8,128)}, f32[1,128,128]{2,1,0:T(8,128)}, f32[1,128,128]{2,1,0:T(8,128)}) custom-call(f32[1,128,128]{2,1,0:T(8,128)} %copy-done.1, f32[1,128,128]{2,1,0:T(8,128)} %copy-done.2, f32[1,128,128]{2,1,0:T(8,128)} %copy-done.3), custom_call_target="tpu_custom_call" | custom-call | tf_op jit(solution)/shard_map/deliver/pallas_call | solution.py:531
Async XLA Ops:
  0.6 1.6 %copy-start = (bf16[2,256,2048]{2,1,0:T(8,128)(2,1)S(1)}, bf16[2,256,2048]{2,1,0:T(8,128)(2,1)}, u32[]{:S(2)}) copy-start(bf16[2,256,2048]{2,1,0:T(8,128)(2,1)} %pixels.1) | copy-start | bytes 6291460
  16.4 0.6 %copy-start.1 = (f32[1,128,128]{2,1,0:T(8,128)}, f32[1,128,128]{2,1,0:T(8,128)S(1)}, u32[]{:S(2)}) copy-start(f32[1,128,128]{2,1,0:T(8,128)S(1)} %get-tuple-element.6.phase) | copy-start | bytes 196612
  17.1 0.6 %copy-start.2 = (f32[1,128,128]{2,1,0:T(8,128)}, f32[1,128,128]{2,1,0:T(8,128)S(1)}, u32[]{:S(2)}) copy-start(f32[1,128,128]{2,1,0:T(8,128)S(1)} %get-tuple-element.7.flux) | copy-start | bytes 196612
  17.7 0.6 %copy-start.3 = (f32[1,128,128]{2,1,0:T(8,128)}, f32[1,128,128]{2,1,0:T(8,128)S(1)}, u32[]{:S(2)}) copy-start(f32[1,128,128]{2,1,0:T(8,128)S(1)} %get-tuple-element.8.spot) | copy-start | bytes 196612
where the time goes:
time: 20.1 us; the launch traced here: 19.9 us
  Pallas kernels  15.8 us (79%)
  local copies, waits for them, and re-layouts  3.46 us (17%)
  between operations  0.66 us (3%)
    pallas_call x1, Pallas kernels, body(): pl.pallas_call(functools.partial(kernel, sizes), out_shape=(square, squar...  14.2 us
    unnamed x8, local copies, waits for them, and re-layouts  3.46 us
    pallas_call x1, Pallas kernels, body(): pl.pallas_call(deliver, out_shape=(square, square, square), in_specs=[vme...  1.6 us

commit v1 on v0

--- a/solution.py
+++ b/solution.py
@@ -74,9 +74,7 @@
     sizes,
     pixels,
     constants,
-    phase,
-    flux,
-    spot,
+    out,
     loaded,
     tables,
     halves,
@@ -202,7 +200,7 @@
     def extra_copy(kind, frame, across):
         return pltpu.make_async_remote_copy(
             src_ref=extras.at[frame, kind, :, square(across)],
-            dst_ref=(flux, spot)[kind].at[0, own_lines, :],
+            dst_ref=out.at[1 + kind, own_lines, :],
             send_sem=extra_sem.at[kind, 0, frame, across],
             recv_sem=extra_sem.at[kind, 1, core, col],
             device_id={"col": across, "sub": frame},
@@ -304,8 +302,8 @@
         halves[0, lines], halves[1, lines] = split_bf16(tables[source_lines])
 
     stripes[seat] = parts[core, :, window(col)]
-    flux[0, own_lines, :] = extras[core, 0, :, square(col)]
-    spot[0, own_lines, :] = extras[core, 1, :, square(col)]
+    out[1, own_lines, :] = extras[core, 0, :, square(col)]
+    out[2, own_lines, :] = extras[core, 1, :, square(col)]
 
     def part_arrival(of_core, of_col):
         return pltpu.make_async_remote_copy(
@@ -320,8 +318,8 @@
     def extra_arrival(kind, of_core, of_col):
         lines = pl.ds(0, high)
         return pltpu.make_async_remote_copy(
-            src_ref=flux.at[0, lines, :],
-            dst_ref=(flux, spot)[kind].at[0, lines, :],
+            src_ref=out.at[1 + kind, lines, :],
+            dst_ref=out.at[1 + kind, lines, :],
             send_sem=extra_sem.at[kind, 0, 0, 0],
             recv_sem=extra_sem.at[kind, 1, of_core, of_col],
             device_id={"col": of_col, "sub": of_core},
@@ -436,7 +434,7 @@
     for copy, _, receives in moves:
         pl.when(receives)(copy.wait_recv)
     mine = mine + side_in[...].T
-    phase[0] = jnp.concatenate(
+    out[0] = jnp.concatenate(
         [
             mine[:MARGIN] + row_in[1, 0] + row_in[1, 1] + row_in[1, 2],
             mine[MARGIN : SUBN - MARGIN],
@@ -461,19 +459,6 @@
     each(blocks, lambda step: sum_copy(step).wait_send())
     for copy, sends, _ in moves:
         pl.when(sends)(copy.wait_send)
-
-
-def deliver(phase, flux, spot, phase_out, flux_out, spot_out, sem):
-    copies = [
-        pltpu.make_async_copy(near, far, sem.at[index])
-        for index, (near, far) in enumerate(
-            ((phase, phase_out), (flux, flux_out), (spot, spot_out))
-        )
-    ]
-    for copy in copies:
-        copy.start()
-    for copy in copies:
-        copy.wait()
 
 
 def body(sizes, pixels):
@@ -485,7 +470,6 @@
     blocks = rows * cols
     vmem = pl.BlockSpec(memory_space=pltpu.VMEM)
     hbm = pl.BlockSpec(memory_space=pltpu.HBM)
-    square = jax.ShapeDtypeStruct((1, SUBN, SUBN), jnp.float32)
     tables = host_tables()
     coarse = coarse_inverse(rows, cols)
     constants = np.zeros((2304, 2 * SUBN), np.float32)
@@ -494,9 +478,9 @@
     dma = pltpu.SemaphoreType.DMA
     results = pl.pallas_call(
         functools.partial(kernel, sizes),
-        out_shape=(square, square, square),
+        out_shape=jax.ShapeDtypeStruct((3, SUBN, SUBN), jnp.float32),
         in_specs=[hbm] * 2,
-        out_specs=(vmem, vmem, vmem),
+        out_specs=vmem,
         scratch_shapes=[
             pltpu.VMEM((frames, pixel_rows, pixel_cols), jnp.bfloat16),
             pltpu.VMEM(tables.shape, jnp.float32),
@@ -524,18 +508,11 @@
             dma((2, 9)),
         ],
         compiler_params=pltpu.CompilerParams(
-            collective_id=0, has_side_effects=True, vmem_limit_bytes=53_000_000
+            collective_id=0, has_side_effects=True, vmem_limit_bytes=53 * 1024 * 1024
         ),
         name="schwarz",
     )(pixels, constants)
-    return pl.pallas_call(
-        deliver,
-        out_shape=(square, square, square),
-        in_specs=[vmem] * 3,
-        out_specs=(hbm, hbm, hbm),
-        scratch_shapes=[dma((3,))],
-        name="deliver",
-    )(*results)
+    return tuple(results[index : index + 1] for index in range(3))
 
 
 def solution(mesh):

time: 20.1 us -> 15.4 us (0.77)
  local copies, waits for them, and re-layouts: 3.46 us -> 0.68 us
  Pallas kernels: 15.8 us -> 13.9 us
    unnamed x8 -> x0, local copies, waits for them, and re-layouts: 3.46 us -> none
    pallas_call x2 -> x1, Pallas kernels: 15.8 us -> 13.9 us  [body(): pl.pallas_call(functools.partial(kernel, sizes), out_shape=jax.ShapeDtype...]
    slice x0 -> x1, local copies, waits for them, and re-layouts: none -> 0.68 us  [body(): return tuple((results[index:index + 1] for index in range(3)))]
where the time goes in v1:
time: 15.4 us; the launch traced here: 15.3 us
  Pallas kernels  13.9 us (90%)
  local copies, waits for them, and re-layouts  0.68 us (4%)
  between operations  0.64 us (4%)
    pallas_call x1, Pallas kernels, body(): pl.pallas_call(functools.partial(kernel, sizes), out_shape=jax.ShapeDtype...  13.9 us
    slice x1, local copies, waits for them, and re-layouts, body(): return tuple((results[index:index + 1] for index in range(3)))  0.68 us

profile of v1, /device:TPU:1, one launch (start us, length us, event | category | flops | bytes accessed | tf_op | source)
XLA Modules:
  0.0 15.3 jit_solution(7021632245040517727)
XLA Ops:
  0.6 13.9 %schwarz.1 = f32[3,128,128]{2,1,0:T(8,128)S(1)} custom-call(bf16[2,256,2048]{2,1,0:T(8,128)(2,1)} %pixels.1, f32[2304,256]{1,0:T(8,128)} %constant.2.clone.constants), custom_call_target="tpu_custom_call" | custom-call | tf_op jit(solution)/shard_map/schwarz/pallas_call | solution.py:479
  14.6 0.7 %fusion = (f32[1,128,128]{2,1,0:T(8,128)}, f32[1,128,128]{2,1,0:T(8,128)}, f32[1,128,128]{2,1,0:T(8,128)}) fusion(f32[3,128,128]{2,1,0:T(8,128)S(1)} %schwarz.1), kind=kLoop, calls=%fused_computation | loop fusion | bytes 393216 | tf_op jit(solution)/shard_map/slice | solution.py:515

commit v2 on v1

--- a/solution.py
+++ b/solution.py
@@ -179,15 +179,12 @@
         0,
     ).astype(jnp.bfloat16)
 
-    def window(across):
-        return pl.ds(pl.multiple_of(across * SUBN, SUBN), 2 * SUBN)
-
     def square(across):
         return pl.ds(pl.multiple_of(across * SUBN, SUBN), SUBN)
 
     def part_copy(frame, across):
         return pltpu.make_async_remote_copy(
-            src_ref=parts.at[frame, :, window(across)],
+            src_ref=parts.at[frame, across, pl.ds(0, high + 2 * MARGIN)],
             dst_ref=stripes.at[seat],
             send_sem=part_sem.at[0, frame, across],
             recv_sem=part_sem.at[1, core, col],
@@ -209,12 +206,12 @@
 
     def edge_copy(which, frame, across):
         lines = (
-            pl.ds(0, MARGIN),
-            pl.ds(high - MARGIN, 2 * MARGIN),
-            pl.ds(high, MARGIN),
+            pl.ds(0, 2 * MARGIN),
+            pl.ds(high, 3 * MARGIN),
+            pl.ds(high + MARGIN, 2 * MARGIN),
         )[which]
         return pltpu.make_async_remote_copy(
-            src_ref=parts.at[frame, lines, window(across)],
+            src_ref=parts.at[frame, across, lines],
             dst_ref=(below, above, second)[which],
             send_sem=edge_sem.at[which, 0, frame, across],
             recv_sem=edge_sem.at[which, 1, 0, 0],
@@ -244,6 +241,7 @@
     line = lax.broadcasted_iota(jnp.int32, (high, wide), 0)
     column = lax.broadcasted_iota(jnp.int32, (high, wide), 1)
     stripe = row * team + seat
+    lane8 = lax.broadcasted_iota(jnp.int32, (MARGIN, SUBN), 1)
     for frame in range(frames):
         summed = []
         for tile in range(cols):
@@ -275,19 +273,32 @@
         carried = jnp.where(line == 0, over, 0.0)[:MARGIN]
         both = jnp.concatenate([source, carried], 0)
         both = jnp.concatenate([both, jnp.zeros((high + MARGIN, SUBN), jnp.float32)], 1)
-        parts[frame] = pltpu.roll(both, MARGIN, 1)
-        if frame == 0:
-            pl.semaphore_wait(barrier, everyone - 1)
+        both = pltpu.roll(both, MARGIN, 1)
+        for across in range(cols):
+            packed = jnp.zeros((MARGIN, SUBN), jnp.float32)
+            for group in range(high // MARGIN + 1):
+                rest = both[
+                    group * MARGIN : (group + 1) * MARGIN,
+                    (across + 1) * SUBN : (across + 2) * SUBN,
+                ]
+                rest = jnp.where(lane8 < 2 * MARGIN, rest, 0.0)
+                packed = packed + (pltpu.roll(rest, 2 * MARGIN * group, 1) if group else rest)
+            parts[frame, across] = jnp.concatenate(
+                [packed, both[:, across * SUBN : (across + 1) * SUBN], packed], 0
+            )
+        extras[frame, 0] = grid(intensity) * (1.0 / (PIX * PIX))
+        extras[frame, 1] = grid(moment_two * scale - slope_x * slope_x - slope_y * slope_y)
+
+    pl.semaphore_wait(barrier, everyone - 1)
+    for frame in range(frames):
         members(frame, lambda across: part_copy(frame, across).start())
-        for which, sends, _ in edges:
-
-            @pl.when(sends)
-            def _():
+    for which, sends, _ in edges:
+
+        @pl.when(sends)
+        def _():
+            for frame in range(frames):
                 for across in range(cols):
                     edge_copy(which, frame, across).start()
-
-        extras[frame, 0] = grid(intensity) * (1.0 / (PIX * PIX))
-        extras[frame, 1] = grid(moment_two * scale - slope_x * slope_x - slope_y * slope_y)
 
     for frame in range(frames):
         for kind in range(2):
@@ -301,7 +312,7 @@
     ):
         halves[0, lines], halves[1, lines] = split_bf16(tables[source_lines])
 
-    stripes[seat] = parts[core, :, window(col)]
+    stripes[seat] = parts[core, col, : high + 2 * MARGIN]
     out[1, own_lines, :] = extras[core, 0, :, square(col)]
     out[2, own_lines, :] = extras[core, 1, :, square(col)]
 
@@ -333,20 +344,28 @@
         def _():
             edge_copy(which, 0, 0).wait_recv()
 
-    top = above[:MARGIN]
-    if high == MARGIN:
-        top = top + second[...]
+    groups = high // MARGIN
+
+    def widen(values, packed, group):
+        rest = pltpu.roll(packed, SUBN - 2 * MARGIN * group, 1) if group else packed
+        return jnp.concatenate([values, rest], 1)
+
+    top = widen(above[:MARGIN], above[2 * MARGIN :], groups - 1)
+    if groups == 1:
+        top = top + widen(second[:MARGIN], second[MARGIN:], groups)
     tiles = [top]
-    carry = above[MARGIN:]
+    carry = widen(above[MARGIN : 2 * MARGIN], above[2 * MARGIN :], groups)
     for index in range(team):
-        tiles.append(stripes[index, :MARGIN] + carry)
-        if high > MARGIN:
-            tiles.append(stripes[index, MARGIN:high])
-        carry = stripes[index, high:]
-    tiles.append(below[...] + carry)
+        packed = stripes[index, :MARGIN]
+        for group in range(groups):
+            lines = stripes[index, (group + 1) * MARGIN : (group + 2) * MARGIN]
+            tile = widen(lines, packed, group)
+            tiles.append(tile if group else tile + carry)
+        carry = widen(stripes[index, high + MARGIN :], packed, groups)
+    tiles.append(widen(below[MARGIN:], below[:MARGIN], 0) + carry)
     total = jnp.concatenate(tiles, 0)
     middle = jnp.sum(total[MARGIN : MARGIN + SUBN].reshape(SUBN // 8, 8, 2 * SUBN), 0)
-    lane = lax.broadcasted_iota(jnp.int32, (8, SUBN), 1)
+    lane = lane8
     sums[block] = jnp.where(lane < MARGIN, middle[:, SUBN:], middle[:, :SUBN])
 
     def sum_copy(step):
@@ -488,12 +507,12 @@
             pltpu.SMEM(coarse.shape, jnp.float32),
             pltpu.VMEM((SUBN * PIX, SUBN), jnp.bfloat16),
             pltpu.VMEM((SUBN * PIX, 2 * SUBN), jnp.bfloat16),
-            pltpu.VMEM((frames, high + MARGIN, wide + SUBN), jnp.float32),
+            pltpu.VMEM((frames, cols, high + 3 * MARGIN, SUBN), jnp.float32),
             pltpu.VMEM((frames, 2, high, wide), jnp.float32),
-            pltpu.VMEM((team, high + MARGIN, 2 * SUBN), jnp.float32),
-            pltpu.VMEM((2 * MARGIN, 2 * SUBN), jnp.float32),
-            pltpu.VMEM((MARGIN, 2 * SUBN), jnp.float32),
-            pltpu.VMEM((MARGIN, 2 * SUBN), jnp.float32),
+            pltpu.VMEM((team, high + 2 * MARGIN, SUBN), jnp.float32),
+            pltpu.VMEM((3 * MARGIN, SUBN), jnp.float32),
+            pltpu.VMEM((2 * MARGIN, SUBN), jnp.float32),
+            pltpu.VMEM((2 * MARGIN, SUBN), jnp.float32),
             pltpu.VMEM((blocks, 8, SUBN), jnp.float32),
             pltpu.VMEM((2 * MARGIN, SUBN), jnp.float32),
             pltpu.VMEM((2, 3, MARGIN, SUBN), jnp.float32),

time: 15.4 us -> 16.3 us (1.058)
  the two profiles are of different devices: /device:TPU:1 before, /device:TPU:0 now
where the time goes in v2:
time: 16.3 us; the launch traced here: 16.2 us
  Pallas kernels  14.9 us (91%)
  local copies, waits for them, and re-layouts  0.68 us (4%)
  between operations  0.64 us (4%)
    pallas_call x1, Pallas kernels, body(): pl.pallas_call(functools.partial(kernel, sizes), out_shape=jax.ShapeDtype...  14.9 us
    slice x1, local copies, waits for them, and re-layouts, body(): return tuple((results[index:index + 1] for index in range(3)))  0.68 us

profile of v2, /device:TPU:0, one launch (start us, length us, event | category | flops | bytes accessed | tf_op | source)
XLA Modules:
  0.0 16.2 jit_solution(11160521855481076603)
XLA Ops:
  0.6 14.9 %schwarz.1 = f32[3,128,128]{2,1,0:T(8,128)S(1)} custom-call(bf16[2,256,2048]{2,1,0:T(8,128)(2,1)} %pixels.1, f32[2304,256]{1,0:T(8,128)} %constant.2.clone.constants), custom_call_target="tpu_custom_call" | custom-call | tf_op jit(solution)/shard_map/schwarz/pallas_call | solution.py:498
  15.5 0.7 %fusion = (f32[1,128,128]{2,1,0:T(8,128)}, f32[1,128,128]{2,1,0:T(8,128)}, f32[1,128,128]{2,1,0:T(8,128)}) fusion(f32[3,128,128]{2,1,0:T(8,128)S(1)} %schwarz.1), kind=kLoop, calls=%fused_computation | loop fusion | bytes 393216 | tf_op jit(solution)/shard_map/slice | solution.py:534

commit v3 on v1

--- a/solution.py
+++ b/solution.py
@@ -28,11 +28,9 @@
 
 def dot_three(left, right, contract=((1,), (0,))):
     (left_high, left_low), (right_high, right_low) = left, right
-    return (
-        dot(left_high, right_high, contract)
-        + dot(left_low, right_high, contract)
-        + dot(left_high, right_low, contract)
-    )
+    count = left_high.shape[0]
+    stacked = dot(jnp.concatenate([left_high, left_low], 0), right_high, contract)
+    return stacked[:count] + stacked[count:] + dot(left_high, right_low, contract)
 
 
 def host_tables():
@@ -255,8 +253,10 @@
             )
         )
         tall = cols * high
-        ones = dot(near, pick_one[...]) + dot(far, pick_one[...])
-        twos = dot(near[:tall], pick_two[...]) + dot(far[:tall], pick_two[...])
+        ones = dot(jnp.concatenate([near, far], 0), pick_one[...])
+        ones = ones[: 3 * tall] + ones[3 * tall :]
+        twos = dot(jnp.concatenate([near[:tall], far[:tall]], 0), pick_two[...])
+        twos = twos[:tall] + twos[tall:]
         intensity = ones[:tall]
         scale = 1.0 / intensity
         slope_x = twos[:, :SUBN] * scale

time: 15.4 us -> 15.4 us (level)
  the two profiles are of different devices: /device:TPU:1 before, /device:TPU:0 now
where the time goes in v3:
time: 15.4 us; the launch traced here: 15.2 us
  Pallas kernels  13.9 us (90%)
  local copies, waits for them, and re-layouts  0.68 us (4%)
  between operations  0.64 us (4%)
    pallas_call x1, Pallas kernels, body(): pl.pallas_call(functools.partial(kernel, sizes), out_shape=jax.ShapeDtype...  13.9 us
    slice x1, local copies, waits for them, and re-layouts, body(): return tuple((results[index:index + 1] for index in range(3)))  0.68 us

profile of v3, /device:TPU:0, one launch (start us, length us, event | category | flops | bytes accessed | tf_op | source)
XLA Modules:
  0.0 15.2 jit_solution(5384274857579626335)
XLA Ops:
  0.6 13.9 %schwarz.1 = f32[3,128,128]{2,1,0:T(8,128)S(1)} custom-call(bf16[2,256,2048]{2,1,0:T(8,128)(2,1)} %pixels.1, f32[2304,256]{1,0:T(8,128)} %constant.2.clone.constants), custom_call_target="tpu_custom_call" | custom-call | tf_op jit(solution)/shard_map/schwarz/pallas_call | solution.py:479
  14.5 0.7 %fusion = (f32[1,128,128]{2,1,0:T(8,128)}, f32[1,128,128]{2,1,0:T(8,128)}, f32[1,128,128]{2,1,0:T(8,128)}) fusion(f32[3,128,128]{2,1,0:T(8,128)S(1)} %schwarz.1), kind=kLoop, calls=%fused_computation | loop fusion | bytes 393216 | tf_op jit(solution)/shard_map/slice | solution.py:515

commit v4 on v2

--- a/solution.py
+++ b/solution.py
@@ -286,19 +286,18 @@
             parts[frame, across] = jnp.concatenate(
                 [packed, both[:, across * SUBN : (across + 1) * SUBN], packed], 0
             )
+        if frame == 0:
+            pl.semaphore_wait(barrier, everyone - 1)
+        members(frame, lambda across: part_copy(frame, across).start())
+        for which, sends, _ in edges:
+
+            @pl.when(sends)
+            def _():
+                for across in range(cols):
+                    edge_copy(which, frame, across).start()
+
         extras[frame, 0] = grid(intensity) * (1.0 / (PIX * PIX))
         extras[frame, 1] = grid(moment_two * scale - slope_x * slope_x - slope_y * slope_y)
-
-    pl.semaphore_wait(barrier, everyone - 1)
-    for frame in range(frames):
-        members(frame, lambda across: part_copy(frame, across).start())
-    for which, sends, _ in edges:
-
-        @pl.when(sends)
-        def _():
-            for frame in range(frames):
-                for across in range(cols):
-                    edge_copy(which, frame, across).start()
 
     for frame in range(frames):
         for kind in range(2):

time: 16.3 us -> 15.3 us (0.939)
  Pallas kernels: 14.9 us -> 13.8 us
    pallas_call x1, Pallas kernels: 14.9 us -> 13.8 us  [body(): pl.pallas_call(functools.partial(kernel, sizes), out_shape=jax.ShapeDtype...]
where the time goes in v4:
time: 15.3 us; the launch traced here: 15.2 us
  Pallas kernels  13.8 us (90%)
  local copies, waits for them, and re-layouts  0.68 us (4%)
  between operations  0.64 us (4%)
    pallas_call x1, Pallas kernels, body(): pl.pallas_call(functools.partial(kernel, sizes), out_shape=jax.ShapeDtype...  13.8 us
    slice x1, local copies, waits for them, and re-layouts, body(): return tuple((results[index:index + 1] for index in range(3)))  0.68 us

profile of v4, /device:TPU:0, one launch (start us, length us, event | category | flops | bytes accessed | tf_op | source)
XLA Modules:
  0.0 15.2 jit_solution(3577819907798668256)
XLA Ops:
  0.6 13.8 %schwarz.1 = f32[3,128,128]{2,1,0:T(8,128)S(1)} custom-call(bf16[2,256,2048]{2,1,0:T(8,128)(2,1)} %pixels.1, f32[2304,256]{1,0:T(8,128)} %constant.2.clone.constants), custom_call_target="tpu_custom_call" | custom-call | tf_op jit(solution)/shard_map/schwarz/pallas_call | solution.py:497
  14.5 0.7 %fusion = (f32[1,128,128]{2,1,0:T(8,128)}, f32[1,128,128]{2,1,0:T(8,128)}, f32[1,128,128]{2,1,0:T(8,128)}) fusion(f32[3,128,128]{2,1,0:T(8,128)S(1)} %schwarz.1), kind=kLoop, calls=%fused_computation | loop fusion | bytes 393216 | tf_op jit(solution)/shard_map/slice | solution.py:533
